TPU v7x, 32 devices: a whole 2x2x4 slice. The times are simulated.
32 devices in a mesh: amp: 8 (over z, x), int: 4 (over y, core).
Axes of the slice: x: 2, y: 2, z: 4, core: 2. Of those that a mesh axis runs over, the one named last changes fastest.
Arguments:
- t2_stored: float32 [1024, 4096], P('amp', 'int'), may hold values from -6 to 6
- integrals: float32 [4096, 4096], P('amp', 'int'), may hold values from -0.09375 to 0.09375
- driver: float32 [1024, 4096], P('amp', 'int'), may hold values from -6 to 6
- eps_occ: float32 [120], replicated, may hold values from -2 to -0.3
- eps_vir: float32 [600], replicated, may hold values from 0.1 to 3
- blk_len: int32 [32], replicated, may hold values from 32 to 128, as said below
- t2_order: int32 [32], replicated, may hold values from 0 to 31, as said below
- int_order: int32 [32], replicated, may hold values from 0 to 31, as said below
Outputs:
- update: float32 [1024, 4096], P('amp', 'int')
Inputs may be any that keep to these rules, and one draw needn't show every extreme that they name: `blk_len`: live slots of a block come first; some block is full and some has 32 live slots. `int_order`: a permutation of the blocks; the integrals' row blocks on one amp index are int_order's blocks of that index. `t2_order`: a permutation of the blocks; the stored column blocks on each int index hold exactly one of the blocks that int_order places on each amp index.
All inputs are finite; a program needn't handle non-finite values.
Results may differ from a plain program's by a relative error of at most 0.00005.
Values sent between devices are 32-bit elements; how exact they have to be, the bound alone decides.
A program may use at most 128 MiB of HBM per device.

v0:
```python
import jax
import jax.numpy as jnp
from jax import lax
from jax.sharding import PartitionSpec as P

NO = 120
NV = 600
TILE = 128


def inverse_of(perm, counter):
    return jnp.sum(jnp.where(perm[None, :] == counter[:, None], counter[None, :], 0), axis=1)


def lookup(table, indices):
    places = jnp.arange(table.shape[0], dtype=jnp.int32)
    return jnp.sum(
        jnp.where(indices[:, None] == places[None, :], table[None, :], jnp.float32(0.0)), axis=1
    )


def on_device(t2_stored, integrals, driver, eps_occ, eps_vir, blk_len, t2_order, int_order):
    row_count = t2_stored.shape[0]
    col_count = integrals.shape[1]
    block_count = blk_len.shape[0]
    owned = integrals.shape[0] // TILE
    per_slice = t2_stored.shape[1] // TILE
    amp_place = lax.axis_index("amp")
    int_place = lax.axis_index("int")
    counter = jnp.arange(block_count, dtype=jnp.int32)
    live_mask = (jnp.arange(TILE, dtype=jnp.int32)[None, :] < blk_len[:, None]).astype(jnp.float32)
    inverse_t2 = inverse_of(t2_order, counter)
    my_blocks = lax.dynamic_slice_in_dim(int_order, amp_place * owned, owned)
    source_block = jnp.take(inverse_t2, my_blocks)
    holder = source_block // per_slice
    all_rows = lax.all_gather(t2_stored, "amp", axis=0, tiled=True)
    here = holder == int_place
    local_pick = jnp.sum(jnp.where(here, source_block % per_slice, 0))
    logical_pick = jnp.sum(jnp.where(here, my_blocks, 0))
    live_row = lax.dynamic_slice_in_dim(live_mask, logical_pick, 1, 0)
    piece = lax.dynamic_slice_in_dim(all_rows, local_pick * TILE, TILE, 1) * live_row
    collected = lax.all_gather(piece, "int", axis=1, tiled=True)
    stacked = collected.reshape(collected.shape[0], owned, TILE)
    amplitudes = jnp.take(stacked, holder, axis=1).reshape(collected.shape[0], owned * TILE)
    summed = lax.psum_scatter(
        jnp.dot(
            amplitudes,
            integrals,
            precision=lax.Precision.HIGHEST,
            preferred_element_type=jnp.float32,
        ),
        "amp",
        scatter_dimension=0,
        tiled=True,
    )
    residual = driver + summed
    row_ids = amp_place * row_count + jnp.arange(row_count, dtype=jnp.int32)
    col_ids = int_place * col_count + jnp.arange(col_count, dtype=jnp.int32)
    occ_first = lookup(eps_occ, row_ids // NO)
    occ_second = lookup(eps_occ, row_ids % NO)
    vir_first = lookup(eps_vir, col_ids % NV)
    vir_second = lookup(eps_vir, (3 * col_ids + col_ids // NV) % NV)
    denominators = (
        vir_first[None, :] + vir_second[None, :] - occ_first[:, None] - occ_second[:, None]
    )
    live_cols = lax.dynamic_slice_in_dim(
        live_mask.reshape(block_count * TILE), int_place * col_count, col_count
    )
    return residual * live_cols[None, :] / denominators


def solution(mesh):
    placed = (P("amp", "int"), P("amp", "int"), P("amp", "int"), P(), P(), P(), P(), P())
    return jax.shard_map(
        on_device, mesh=mesh, in_specs=placed, out_specs=P("amp", "int"), check_vma=False
    )
```

profile of v0, /device:TPU:0, one launch (start us, length us, event | category | flops | bytes accessed | tf_op | source)
XLA Modules:
  0.0 226.4 jit_solution(14133576417330878228)
XLA Ops:
  6.5 0.0 copy-start
  6.5 0.0 all-gather.3.cloned.1.call-start
  6.5 2.2 copy.12
  8.7 0.0 all-gather.3.cloned.1.call-update
  8.8 0.0 all-gather.5.cloned.1.call-start
  8.8 0.7 compare_select_fusion.1
  9.6 0.8 select_reduce_fusion.4
  10.3 0.6 gather_fusion
  11.0 0.0 copy-done.3
  11.0 0.1 compare_and_fusion
  11.1 0.7 fusion.9
  14.3 0.0 copy-done.4
  14.3 0.1 fusion.1
  14.4 72.8 %all-gather.3.cloned.1.call-done = f32[1024,1024]{0,1:T(8,128)} async-done(((f32[128,1024]{0,1:T(8,128)}), f32[1024,1024]{0,1:T(8,128)}) %all-gather.3.cloned.1.call-update) | async-done | bytes 4194320 | tf_op jit(solution)/shard_map/all_gather | solution.py:36
  87.2 1.9 dynamic-slice_multiply_fusion
  89.1 0.0 all-gather.5.cloned.1.call-update
  89.1 0.0 reduce-scatter.2.cloned.1.call-start
  89.2 0.1 broadcast_bitcast_fusion
  89.3 20.8 %all-gather.5.cloned.1.call-done = f32[1024,512]{0,1:T(8,128)} async-done(((f32[1024,128]{0,1:T(8,128)}), f32[1024,512]{0,1:T(8,128)}) %all-gather.5.cloned.1.call-update) | async-done | bytes 2097168 | tf_op jit(solution)/shard_map/all_gather | solution.py:42
  110.0 2.9 %copy.13 = f32[1024,4,128]{2,0,1:T(8,128)} copy(f32[1024,4,128]{0,2,1:T(8,128)} %bitcast.13) | data formatting | bytes 4194304 | tf_op jit(solution)/shard_map/reshape | solution.py:43
  113.0 3.6 %gather_fusion.1 = f32[4,1024,128]{2,1,0:T(8,128)} fusion(f32[1024,4,128]{2,0,1:T(8,128)} %copy.13, s32[1024]{0:T(1024)S(1)} %pad_clamp_fusion), kind=kCustom, calls=%fused_computation.1 | custom fusion | bytes 4194320 | tf_op jit(solution)/shard_map/jit(_take)/gather | solution.py:44
  116.6 2.9 %copy.14 = f32[1024,4,128]{0,2,1:T(8,128)} copy(f32[1024,4,128]{2,0,1:T(8,128)} %bitcast.12) | data formatting | bytes 4194304 | tf_op jit(solution)/shard_map/jit(_take)/gather | solution.py:44
  119.5 1.8 bitcast_select_fusion
  121.3 0.0 copy-done
  121.3 8.4 %fusion.12 = f32[1024,1024]{1,0:T(8,128)} fusion(f32[1024,512]{0,1:T(8,128)S(1)} %bitcast_select_fusion, f32[512,1024]{1,0:T(8,128)S(1)} %copy-done), kind=kOutput, calls=%fused_computation.51 | convolution fusion | flops 6442450944 | bytes 8388608 | tf_op jit(solution)/shard_map/dot_general | solution.py:46
  129.7 0.0 reduce-scatter.2.cloned.1.call-update
  129.8 0.6 copy-done.2
  130.4 0.6 select_reduce_fusion
  131.1 0.1 select_reduce_fusion.3
  131.2 86.6 %reduce-scatter.2.cloned.1.call-done = f32[128,1024]{1,0:T(8,128)} async-done(((f32[1024,1024]{1,0:T(8,128)}), f32[128,1024]{1,0:T(8,128)}) %reduce-scatter.2.cloned.1.call-update) | async-done | bytes 524304 | tf_op jit(solution)/shard_map/reduce_scatter | solution.py:45
  217.8 0.0 copy-done.1
  217.8 2.0 subtract_divide_fusion
  (13 shorter events, 0.1 us)
Async XLA Ops:
  6.5 114.8 %copy-start = (f32[512,1024]{1,0:T(8,128)S(1)}, f32[512,1024]{1,0:T(8,128)}, u32[]{:S(2)}) copy-start(f32[512,1024]{1,0:T(8,128)} %param.9) | copy-start | bytes 6291460
  6.5 4.4 %copy-start.3 = (s32[32]{0:T(128)S(1)}, s32[32]{0:T(128)}, u32[]{:S(2)}) copy-start(s32[32]{0:T(128)} %param.15) | copy-start | bytes 388
  6.5 7.7 %copy-start.4 = (s32[32]{0:T(128)S(1)}, s32[32]{0:T(128)}, u32[]{:S(2)}) copy-start(s32[32]{0:T(128)} %param.13) | copy-start | bytes 388
  6.5 80.6 %all-gather.3.cloned.1.call-start = ((), (), s32[]{:S(2)}) async-start(), calls=%async_computation.1 | async-start | bytes 4718592 | tf_op jit(solution)/shard_map/all_gather | solution.py:36
  8.8 101.3 %all-gather.5.cloned.1.call-start = ((), (), s32[]{:S(2)}) async-start(), calls=%async_computation.2 | async-start | bytes 2621440 | tf_op jit(solution)/shard_map/all_gather | solution.py:42
  89.1 128.7 %reduce-scatter.2.cloned.1.call-start = ((), (), s32[]{:S(2)}) async-start(), calls=%async_computation.3 | async-start | bytes 4718592 | tf_op jit(solution)/shard_map/reduce_scatter | solution.py:45
  129.7 0.7 copy-start.2
  129.7 1.4 copy-start.5
  129.7 88.1 %copy-start.1 = (f32[128,1024]{1,0:T(8,128)S(1)}, f32[128,1024]{1,0:T(8,128)}, u32[]{:S(2)}) copy-start(f32[128,1024]{1,0:T(8,128)} %param.10) | copy-start | bytes 1572868
Sparse Core Ops, SparseCore 0:
  9.4 77.7 all-gather.2
  89.2 20.7 all-gather.4
  129.9 87.9 reduce-scatter.1
where the time goes:
time: 227 us; the launch traced here: 226 us
  waiting for transfers between devices  180 us (79%)
  between operations  15.7 us (7%)
  local copies, waits for them, and re-layouts  13 us (6%)
  other arithmetic  8.96 us (4%)
  matrix products  8.4 us (4%)
    reduce_scatter x1, waiting for transfers between devices, on_device(): lax.psum_scatter(jnp.dot(amplitudes, integrals, precision=lax.Precision.H...  86.6 us
    all_gather x1, waiting for transfers between devices, on_device(): all_rows = lax.all_gather(t2_stored, 'amp', axis=0, tiled=True)  72.8 us
    all_gather x1, waiting for transfers between devices, on_device(): collected = lax.all_gather(piece, 'int', axis=1, tiled=True)  20.8 us
    dot_general x1, matrix products, on_device(): jnp.dot(amplitudes, integrals, precision=lax.Precision.HIGHEST, preferred...  8.4 us
    gather x2, local copies, waits for them, and re-layouts, on_device(): jnp.take(stacked, holder, axis=1).reshape(collected.shape[0], owned * TILE)  6.51 us
  transfers between devices with their start and end apart: 3, of which 3 were waited for; matrix products, arithmetic and copies ran while one was open for 2% of the time, Pallas kernels for 0%

commit v1 on v0

--- a/solution.py
+++ b/solution.py
@@ -39,7 +39,8 @@
     logical_pick = jnp.sum(jnp.where(here, my_blocks, 0))
     live_row = lax.dynamic_slice_in_dim(live_mask, logical_pick, 1, 0)
     piece = lax.dynamic_slice_in_dim(all_rows, local_pick * TILE, TILE, 1) * live_row
-    collected = lax.all_gather(piece, "int", axis=1, tiled=True)
+    sent = jnp.stack([piece] * lax.axis_size("int"))
+    collected = jnp.concatenate(lax.all_to_all(sent, "int", 0, 0), axis=1)
     stacked = collected.reshape(collected.shape[0], owned, TILE)
     amplitudes = jnp.take(stacked, holder, axis=1).reshape(collected.shape[0], owned * TILE)
     summed = lax.psum_scatter(

time: 227 us -> 230 us (1.013)
  starting transfers between devices: 0.09 us -> 4.48 us
  local copies, waits for them, and re-layouts: 13 us -> 9.31 us
    all_to_all x0 -> x1, waiting for transfers between devices: none -> 25.6 us  [on_device(): collected = jnp.concatenate(lax.all_to_all(sent, 'int', 0, 0), axis=1)]
    all_gather x1 -> x0, waiting for transfers between devices: 20.8 us -> none  [on_device(): collected = lax.all_gather(piece, 'int', axis=1, tiled=True)]
    all_to_all x0 -> x1, starting transfers between devices: none -> 4.44 us  [on_device(): collected = jnp.concatenate(lax.all_to_all(sent, 'int', 0, 0), axis=1)]
    reshape x1 -> x0, local copies, waits for them, and re-layouts: 2.94 us -> none  [on_device(): stacked = collected.reshape(collected.shape[0], owned, TILE)]
    reduce_scatter x1, waiting for transfers between devices: 86.6 us -> 84 us  [on_device(): lax.psum_scatter(jnp.dot(amplitudes, integrals, precision=lax.Precision.H...]
  transfers between devices with their start and end apart: 3 -> 3, of which waited for: 3 -> 3; matrix products, arithmetic and copies ran while one was open for 2% -> 3% of each run, Pallas kernels for 0% -> 0%
where the time goes in v1:
time: 230 us; the launch traced here: 229 us
  waiting for transfers between devices  181 us (79%)
  between operations  16.1 us (7%)
  other arithmetic  10 us (4%)
  local copies, waits for them, and re-layouts  9.31 us (4%)
  matrix products  8.4 us (4%)
  starting transfers between devices  4.48 us (2%)
    reduce_scatter x1, waiting for transfers between devices, on_device(): lax.psum_scatter(jnp.dot(amplitudes, integrals, precision=lax.Precision.H...  84 us
    all_gather x1, waiting for transfers between devices, on_device(): all_rows = lax.all_gather(t2_stored, 'amp', axis=0, tiled=True)  70.8 us
    all_to_all x1, waiting for transfers between devices, on_device(): collected = jnp.concatenate(lax.all_to_all(sent, 'int', 0, 0), axis=1)  25.6 us
    dot_general x1, matrix products, on_device(): jnp.dot(amplitudes, integrals, precision=lax.Precision.HIGHEST, preferred...  8.4 us
    gather x2, local copies, waits for them, and re-layouts, on_device(): jnp.take(stacked, holder, axis=1).reshape(collected.shape[0], owned * TILE)  6.51 us
  transfers between devices with their start and end apart: 3, of which 3 were waited for; matrix products, arithmetic and copies ran while one was open for 3% of the time, Pallas kernels for 0%

profile of v1, /device:TPU:0, one launch (start us, length us, event | category | flops | bytes accessed | tf_op | source)
XLA Modules:
  0.0 229.4 jit_solution(1337309586038898925)
XLA Ops:
  6.5 0.0 copy-start
  6.5 0.0 all-gather.2.cloned.1.call-start
  6.5 0.7 all-gather.2.cloned.1.call-update
  7.3 0.7 compare_select_fusion.1
  8.0 0.8 select_reduce_fusion.4
  8.8 0.6 gather_fusion
  9.4 0.7 compare_and_fusion
  10.2 1.4 fusion.9
  14.1 0.7 fusion.1
  14.8 70.8 %all-gather.2.cloned.1.call-done = f32[1024,1024]{1,0:T(8,128)} async-done(((f32[128,1024]{1,0:T(8,128)}), f32[1024,1024]{1,0:T(8,128)}) %all-gather.2.cloned.1.call-update) | async-done | bytes 4194320 | tf_op jit(solution)/shard_map/all_gather | solution.py:36
  85.6 1.1 dynamic-slice_multiply_fusion
  86.7 1.4 stack.2
  88.1 4.4 %all-to-all-start = ((f32[4,1024,128]{2,1,0:T(8,128)}), f32[4,1024,128]{2,1,0:T(8,128)}, u32[]{:S(2)}, u32[]{:S(2)}) async-start(f32[4,1024,128]{2,1,0:T(8,128)} %stack.2), calls=%async_computation | async-start | bytes 4194304 | tf_op jit(solution)/shard_map/all_to_all | solution.py:43
  92.6 0.0 reduce-scatter.2.cloned.1.call-start
  92.6 0.1 broadcast_bitcast_fusion
  92.7 25.6 %all-to-all-done = f32[4,1024,128]{2,1,0:T(8,128)} async-done(((f32[4,1024,128]{2,1,0:T(8,128)}), f32[4,1024,128]{2,1,0:T(8,128)}, u32[]{:S(2)}, u32[]{:S(2)}) %all-to-all-start) | async-done | bytes 2097184 | tf_op jit(solution)/shard_map/all_to_all | solution.py:43
  118.3 3.6 %gather_fusion.1 = f32[4,1024,128]{2,1,0:T(8,128)} fusion(f32[1024,4,128]{2,0,1:T(8,128)} %bitcast.2, s32[1024]{0:T(1024)S(1)} %pad_clamp_fusion), kind=kCustom, calls=%fused_computation.1 | custom fusion | bytes 4194320 | tf_op jit(solution)/shard_map/jit(_take)/gather | solution.py:45
  121.9 2.9 %copy.10 = f32[1024,4,128]{0,2,1:T(8,128)} copy(f32[1024,4,128]{2,0,1:T(8,128)} %bitcast.12) | data formatting | bytes 4194304 | tf_op jit(solution)/shard_map/jit(_take)/gather | solution.py:45
  124.8 1.8 bitcast_select_fusion
  126.6 0.0 copy-done
  126.7 8.4 %fusion.12 = f32[1024,1024]{1,0:T(8,128)} fusion(f32[1024,512]{0,1:T(8,128)S(1)} %bitcast_select_fusion, f32[512,1024]{1,0:T(8,128)S(1)} %copy-done), kind=kOutput, calls=%fused_computation.51 | convolution fusion | flops 6442450944 | bytes 8388608 | tf_op jit(solution)/shard_map/dot_general | solution.py:47
  135.1 0.0 copy-start.2
  135.1 0.0 copy-start.3
  135.1 0.0 copy-start.1
  135.1 0.0 reduce-scatter.2.cloned.1.call-update
  135.1 0.6 copy-done.2
  135.7 0.6 select_reduce_fusion
  136.5 0.0 copy-done.3
  136.5 0.1 select_reduce_fusion.3
  136.6 84.0 %reduce-scatter.2.cloned.1.call-done = f32[128,1024]{1,0:T(8,128)} async-done(((f32[1024,1024]{1,0:T(8,128)}), f32[128,1024]{1,0:T(8,128)}) %reduce-scatter.2.cloned.1.call-update) | async-done | bytes 524304 | tf_op jit(solution)/shard_map/reduce_scatter | solution.py:46
  220.5 0.0 copy-done.1
  220.5 2.0 subtract_divide_fusion
  (7 shorter events, 0.1 us)
Async XLA Ops:
  6.5 120.1 %copy-start = (f32[512,1024]{1,0:T(8,128)S(1)}, f32[512,1024]{1,0:T(8,128)}, u32[]{:S(2)}) copy-start(f32[512,1024]{1,0:T(8,128)} %param.9) | copy-start | bytes 6291460
  6.5 79.1 %all-gather.2.cloned.1.call-start = ((), (), s32[]{:S(2)}) async-start(), calls=%async_computation.2 | async-start | bytes 4718592 | tf_op jit(solution)/shard_map/all_gather | solution.py:36
  88.1 30.2 %all-to-all-start = ((f32[4,1024,128]{2,1,0:T(8,128)}), f32[4,1024,128]{2,1,0:T(8,128)}, u32[]{:S(2)}, u32[]{:S(2)}) async-start(f32[4,1024,128]{2,1,0:T(8,128)} %stack.2), calls=%async_computation | async-start | bytes 4194304 | tf_op jit(solution)/shard_map/all_to_all | solution.py:43
  92.6 127.9 %reduce-scatter.2.cloned.1.call-start = ((), (), s32[]{:S(2)}) async-start(), calls=%async_computation.3 | async-start | bytes 4718592 | tf_op jit(solution)/shard_map/reduce_scatter | solution.py:46
  135.1 0.7 copy-start.2
  135.1 1.4 copy-start.3
  135.1 85.4 %copy-start.1 = (f32[128,1024]{1,0:T(8,128)S(1)}, f32[128,1024]{1,0:T(8,128)}, u32[]{:S(2)}) copy-start(f32[128,1024]{1,0:T(8,128)} %param.10) | copy-start | bytes 1572868
Sparse Core Ops, SparseCore 0:
  9.5 76.0 all-gather.1
  135.2 85.2 reduce-scatter.1
